TPU v7x, 32 devices: a whole 2x2x4 slice. The times are simulated.
32 devices in a mesh: grp: 2 (over y), freq: 4 (over z), ell: 2 (over x), pol: 2 (over core).
Axes of the slice: x: 2, y: 2, z: 4, core: 2. Of those that a mesh axis runs over, the one named last changes fastest.
Arguments:
- beam_matrix: bfloat16 [8, 2, 512, 8192], P(('grp', 'freq'), None, None, ('ell', 'pol')), parts along dimension 0, may hold values from -0.375 to 0.375
- sky_spectrum: float32 [8, 3, 8192], P(('grp', 'freq'), None, ('ell', 'pol')), parts along dimension 0, may hold values from 0.1 to 10
- taper_tiles: bfloat16 [3, 512, 512], P(None, ('ell', 'pol')), may hold values from 0.5 to 1.5
- noise_tiles: bfloat16 [8, 3, 512, 2, 512], P(('grp', 'freq'), None, ('ell', 'pol')), parts along dimension 0, may hold values from -4 to 4
Outputs:
- covariance: float32 [8, 3, 512, 2, 512], P(('grp', 'freq'), None, ('ell', 'pol')), parts along dimension 0
There are 2 independent parts, one for each index of `grp`. A program takes and returns all parts, laid end to end along the dimension named above; an argument that names none is the same for every part. Nothing has to cross between parts.
All inputs are finite; a program needn't handle non-finite values.
Results may differ from a plain program's by a relative error of at most 0.012.
Values may be sent and summed in bfloat16 or wider, within the bound.
No kernel may reach another device: no remote copies, remote signals or barrier semaphores. Data moves between devices by JAX's collectives and lax.ppermute only.
A program may use at most 64 MiB of HBM per device.

v0:
```python
import jax
import jax.numpy as jnp
from jax import lax
from jax.sharding import PartitionSpec as P


def passed_along(block, axis, distance):
    devices = range(lax.axis_size(axis))
    route = [(i - distance, i) for i in devices if i - distance in devices]
    return lax.ppermute(block, axis, route)


def make_term(scaled, stacked_right, mode_count):

    def tile_term(first_row, row_count):
        real_rows = scaled[0]
        imag_rows = scaled[1]
        top_half = jnp.concatenate([real_rows, imag_rows], axis=-1)
        bottom_half = jnp.concatenate([imag_rows, -real_rows], axis=-1)
        left_rows = jnp.stack([top_half, bottom_half], axis=1).reshape(
            2 * row_count, top_half.shape[-1]
        )
        product = lax.dot_general(
            left_rows, stacked_right, (((1,), (1,)), ((), ())), preferred_element_type=jnp.float32
        )
        return product.reshape(row_count, 2, mode_count)

    return tile_term


def local(beam_matrix, sky_spectrum, taper_tiles, noise_tiles):
    per_device = beam_matrix.shape[0]
    mode_count = beam_matrix.shape[2]
    separations = sky_spectrum.shape[1]
    local_rows = taper_tiles.shape[1]
    needed = (per_device - 1 + separations) // per_device
    blocks = [beam_matrix]
    for offset in range(needed):
        blocks.append(passed_along(beam_matrix, "freq", -(offset + 1)))
    term_list = []
    for sep_index in range(separations):
        target = sep_index + 1
        partner = blocks[target // per_device][target % per_device]
        spec_row = sky_spectrum[0, sep_index]
        scaled = (spec_row[None, None, :] * beam_matrix[0].astype(jnp.float32)).astype(jnp.bfloat16)
        stacked_right = jnp.concatenate([partner[0], partner[1]], axis=-1)
        tile_term = make_term(scaled, stacked_right, mode_count)
        term_list.append(
            lax.psum_scatter(
                tile_term(jnp.int32(0), lax.axis_size(("ell", "pol")) * local_rows).astype(
                    jnp.bfloat16
                ),
                ("ell", "pol"),
                scatter_dimension=0,
                tiled=True,
            ).astype(jnp.float32)
        )
    summed = jnp.stack(term_list).reshape(per_device, separations, local_rows, 2, mode_count)
    result = taper_tiles.astype(jnp.float32)[None, :, :, None, :] * summed + noise_tiles.astype(
        jnp.float32
    )
    return result


def solution(mesh):
    placed = (
        P(("grp", "freq"), None, None, ("ell", "pol")),
        P(("grp", "freq"), None, ("ell", "pol")),
        P(None, ("ell", "pol"), None),
        P(("grp", "freq"), None, ("ell", "pol"), None, None),
    )
    return jax.shard_map(
        local,
        mesh=mesh,
        in_specs=placed,
        out_specs=P(("grp", "freq"), None, ("ell", "pol"), None, None),
        check_vma=False,
    )
```

profile of v0, /device:TPU:0, one launch (start us, length us, event | category | flops | bytes accessed | tf_op | source)
XLA Modules:
  0.0 442.2 jit_solution(7819483632951395245)
XLA Ops:
  6.5 1.3 collective-permute-start
  7.8 1.3 collective-permute-start.1
  9.1 1.3 collective-permute-start.2
  10.4 0.7 fusion.36
  11.2 4.6 %fusion = (bf16[2,512,2048]{2,1,0:T(8,128)(2,1)S(1)}, bf16[2,512,2048]{2,1,0:T(8,128)(2,1)S(1)}, bf16[2,512,2048]{2,1,0:T(8,128)(2,1)S(1)}) fusion(bf16[1,2,512,2048]{3,2,1,0:T(8,128)(2,1)} %param.4, f32[2048]{0:T(1024)S(1)} %bitcast.71, f32[2048]{0:T(1024)S(1)} %bitcast.72, f32[2048]{0:T(1024)S(1)} %bitcast.73), kind=kLoop, calls=%fused_computation.3 | loop fusion | flops 14680064 | bytes 16801792 | tf_op jit(solution)/shard_map/convert_element_type | solution.py:45
  15.8 0.3 fusion.33
  16.1 0.6 slice_bitcast_fusion.11
  16.7 1.0 maximum_bitcast_fusion
  17.7 0.5 copy-done
  18.2 3.4 slice_bitcast_fusion.3
  21.6 80.6 %collective-permute-done = bf16[1,2,512,2048]{3,2,1,0:T(8,128)(2,1)S(1)} collective-permute-done((bf16[1,2,512,2048]{3,2,1,0:T(8,128)(2,1)}, bf16[1,2,512,2048]{3,2,1,0:T(8,128)(2,1)S(1)}, u32[]{:S(2)}, u32[]{:S(2)}) %collective-permute-start) | collective-permute-done | bytes 4194336 | tf_op jit(solution)/shard_map/ppermute | solution.py:10
  102.2 0.6 slice_bitcast_fusion.9
  102.8 5.5 %fusion.27 = bf16[512,2,512]{2,0,1:T(8,128)(2,1)} fusion(bf16[512,2048]{1,0:T(8,128)(2,1)S(1)} %get-tuple-element.11, bf16[512,2048]{1,0:T(8,128)(2,1)S(1)} %get-tuple-element.10, bf16[512,1,4096]{2,0,1:T(8,128)(2,1)S(1)} %get-tuple-element.21, bf16[512,1,4096]{2,0,1:T(8,128)(2,1)S(1)} %get-tuple-element.20), kind=kOutput, calls=%fused_computation.48 | convolution fusion | flops 4308074496 | bytes 13631488 | tf_op jit(solution)/shard_map/dot_general | solution.py:23
  108.3 0.0 reduce-scatter.4.cloned.1.call-update
  108.3 0.0 reduce-scatter.6.cloned.1.call-start
  108.4 3.3 maximum_bitcast_fusion.4
  111.7 0.7 copy-done.1
  112.5 0.1 fusion.35
  112.6 260.6 %collective-permute-done.1 = bf16[1,2,512,2048]{3,2,1,0:T(8,128)(2,1)} collective-permute-done((bf16[1,2,512,2048]{3,2,1,0:T(8,128)(2,1)}, bf16[1,2,512,2048]{3,2,1,0:T(8,128)(2,1)}, u32[]{:S(2)}, u32[]{:S(2)}) %collective-permute-start.1) | collective-permute-done | bytes 4194336 | tf_op jit(solution)/shard_map/ppermute | solution.py:10
  373.2 2.5 slice_bitcast_fusion.5
  375.7 5.5 %fusion.24 = bf16[512,2,512]{2,0,1:T(8,128)(2,1)} fusion(bf16[512,2048]{1,0:T(8,128)(2,1)S(1)} %get-tuple-element.15, bf16[512,2048]{1,0:T(8,128)(2,1)S(1)} %get-tuple-element.14, bf16[512,1,4096]{2,0,1:T(8,128)(2,1)S(1)} %get-tuple-element.23, bf16[512,1,4096]{2,0,1:T(8,128)(2,1)S(1)} %get-tuple-element.22), kind=kOutput, calls=%fused_computation.47 | convolution fusion | flops 4308074496 | bytes 13631488 | tf_op jit(solution)/shard_map/dot_general | solution.py:23
  381.2 0.0 reduce-scatter.6.cloned.1.call-update
  381.2 0.2 reduce-scatter.8.cloned.1.call-start
  381.4 3.2 maximum_bitcast_fusion.8
  384.6 2.6 slice_bitcast_fusion.1
  387.3 5.5 %fusion.21 = bf16[512,2,512]{2,0,1:T(8,128)(2,1)} fusion(bf16[512,2048]{1,0:T(8,128)(2,1)S(1)} %get-tuple-element.19, bf16[512,2048]{1,0:T(8,128)(2,1)S(1)} %get-tuple-element.18, bf16[512,1,4096]{2,0,1:T(8,128)(2,1)S(1)} %get-tuple-element.25, bf16[512,1,4096]{2,0,1:T(8,128)(2,1)S(1)} %get-tuple-element.24), kind=kOutput, calls=%fused_computation.46 | convolution fusion | flops 4308074496 | bytes 13631488 | tf_op jit(solution)/shard_map/dot_general | solution.py:23
  392.8 0.1 convert_element_type.35
  392.9 0.0 reduce-scatter.4.cloned.1.call-done
  392.9 11.5 %reduce-scatter.6.cloned.1.call-done = bf16[128,2,512]{2,0,1:T(8,128)(2,1)} async-done(((bf16[512,2,512]{2,0,1:T(8,128)(2,1)}), bf16[128,2,512]{2,0,1:T(8,128)(2,1)}) %reduce-scatter.6.cloned.1.call-update) | async-done | bytes 262160 | tf_op jit(solution)/shard_map/reduce_scatter | solution.py:49
  404.5 27.5 %reduce-scatter.8.cloned.1.call-done = bf16[128,2,512]{2,0,1:T(8,128)(2,1)} async-done(((bf16[512,2,512]{2,0,1:T(8,128)(2,1)}), bf16[128,2,512]{2,0,1:T(8,128)(2,1)}) %reduce-scatter.8.cloned.1.call-update) | async-done | bytes 262160 | tf_op jit(solution)/shard_map/reduce_scatter | solution.py:49
  431.9 1.4 convert_add_fusion
  433.3 2.4 copy.6
  (9 shorter events, 0.0 us)
Async XLA Ops:
  6.5 386.4 %reduce-scatter.4.cloned.1.call-start = ((), (), s32[]{:S(2)}) async-start(), calls=%async_computation.3 | async-start | bytes 1310720 | tf_op jit(solution)/shard_map/reduce_scatter | solution.py:49
  6.5 95.7 %collective-permute-start = (bf16[1,2,512,2048]{3,2,1,0:T(8,128)(2,1)}, bf16[1,2,512,2048]{3,2,1,0:T(8,128)(2,1)S(1)}, u32[]{:S(2)}, u32[]{:S(2)}) collective-permute-start(bf16[1,2,512,2048]{3,2,1,0:T(8,128)(2,1)} %param.4), channel_id=1, source_target_pairs={{4,0},{8,4},{12,8},{5,1},{9,5},{13,9},{6,2},{10,6},{14,10},{7,3},{... | collective-permute-start | bytes 12582920 | tf_op jit(solution)/shard_map/ppermute | solution.py:10
  7.8 365.3 %collective-permute-start.1 = (bf16[1,2,512,2048]{3,2,1,0:T(8,128)(2,1)}, bf16[1,2,512,2048]{3,2,1,0:T(8,128)(2,1)}, u32[]{:S(2)}, u32[]{:S(2)}) collective-permute-start(bf16[1,2,512,2048]{3,2,1,0:T(8,128)(2,1)} %param.4), channel_id=1, source_target_pairs={{8,0},{12,4},{9,1},{13,5},{10,2},{14,6},{11,3},{15,7},{24,16},{28,... | collective-permute-start | bytes 12582920 | tf_op jit(solution)/shard_map/ppermute | solution.py:10
  9.1 375.5 %collective-permute-start.2 = (bf16[1,2,512,2048]{3,2,1,0:T(8,128)(2,1)}, bf16[1,2,512,2048]{3,2,1,0:T(8,128)(2,1)}, u32[]{:S(2)}, u32[]{:S(2)}) collective-permute-start(bf16[1,2,512,2048]{3,2,1,0:T(8,128)(2,1)} %param.4), channel_id=1, source_target_pairs={{12,0},{13,1},{14,2},{15,3},{28,16},{29,17},{30,18},{31,19}} | collective-permute-start | bytes 12582920 | tf_op jit(solution)/shard_map/ppermute | solution.py:10
  15.8 2.4 copy-start
  108.3 296.1 %reduce-scatter.6.cloned.1.call-start = ((), (), s32[]{:S(2)}) async-start(), calls=%async_computation.4 | async-start | bytes 1310720 | tf_op jit(solution)/shard_map/reduce_scatter | solution.py:49
  108.4 4.1 copy-start.1
  381.2 50.7 %reduce-scatter.8.cloned.1.call-start = ((), (), s32[]{:S(2)}) async-start(), calls=%async_computation.5 | async-start | bytes 1310720 | tf_op jit(solution)/shard_map/reduce_scatter | solution.py:49
  387.3 5.5 %copy-start.3 = (bf16[3,128,512]{2,1,0:T(8,128)(2,1)S(1)}, bf16[3,128,512]{2,1,0:T(8,128)(2,1)}, u32[]{:S(2)}) copy-start(bf16[3,128,512]{2,1,0:T(8,128)(2,1)} %param.6) | copy-start | bytes 1179652
  387.3 44.6 %copy-start.2 = (bf16[1,3,128,2,512]{4,3,2,1,0:T(2,128)(2,1)S(1)}, bf16[1,3,128,2,512]{4,3,2,1,0:T(2,128)(2,1)}, u32[]{:S(2)}) copy-start(bf16[1,3,128,2,512]{4,3,2,1,0:T(2,128)(2,1)} %param.7) | copy-start | bytes 2359300
Sparse Core Ops, SparseCore 0:
  108.5 205.1 reduce-scatter.3
  381.3 23.0 reduce-scatter.5
  407.0 24.8 reduce-scatter.7
where the time goes:
time: 443 us; the launch traced here: 442 us
  waiting for transfers between devices  380 us (86%)
  matrix products  16.5 us (4%)
  local copies, waits for them, and re-layouts  14 us (3%)
  other arithmetic  14 us (3%)
  between operations  13.3 us (3%)
    ppermute x3, waiting for transfers between devices, passed_along(): return lax.ppermute(block, axis, route)  341 us
    reduce_scatter x3, waiting for transfers between devices, local(): lax.psum_scatter(tile_term(jnp.int32(0), lax.axis_size(('ell', 'pol')) *...  39 us
    dot_general x3, matrix products, tile_term(): lax.dot_general(left_rows, stacked_right, (((1,), (1,)), ((), ())), prefe...  16.5 us
  transfers between devices with their start and end apart: 6, of which 4 were waited for; matrix products, arithmetic and copies ran while one was open for 9% of the time, Pallas kernels for 0%

commit v1 on v0

v1 whole, which is shorter than its diff:
```python
import jax
import jax.numpy as jnp
from jax import lax
from jax.experimental import pallas as pl
from jax.experimental.pallas import tpu as pltpu
from jax.sharding import PartitionSpec as P

LANES = 128
DOWN, UP = 0, 1
LOW, HIGH = 1, 2


def passed_along(block, axis, distance):
    devices = range(lax.axis_size(axis))
    route = [(i - distance, i) for i in devices if i - distance in devices]
    return lax.ppermute(block, axis, route)


def tile_term(scaled, stacked_right):
    real_rows, imag_rows = scaled[0], scaled[1]
    top_half = jnp.concatenate([real_rows, imag_rows], axis=-1)
    bottom_half = jnp.concatenate([imag_rows, -real_rows], axis=-1)
    rows = real_rows.shape[0]
    left_rows = jnp.stack([top_half, bottom_half], axis=1).reshape(2 * rows, -1)
    product = lax.dot_general(
        left_rows, stacked_right, (((1,), (1,)), ((), ())), preferred_element_type=jnp.float32
    )
    return product.reshape(rows, 2, -1)


def partners_passed_down(beam_matrix, sky_spectrum, taper_tiles, noise_tiles):
    separations = sky_spectrum.shape[1]
    terms = []
    for sep in range(separations):
        partner = passed_along(beam_matrix, "freq", -(sep + 1))[0]
        scaled = sky_spectrum[0, sep][None, None, :] * beam_matrix[0].astype(jnp.float32)
        right = jnp.concatenate([partner[0], partner[1]], axis=-1)
        term = tile_term(scaled.astype(jnp.bfloat16), right).astype(jnp.bfloat16)
        term = lax.psum_scatter(term, ("ell", "pol"), scatter_dimension=0, tiled=True)
        terms.append(term.astype(jnp.float32))
    summed = jnp.stack(terms)[None]
    taper = taper_tiles.astype(jnp.float32)[None, :, :, None, :]
    return taper * summed + noise_tiles.astype(jnp.float32)


def products_body(steps, columns, cores, place_ref, spec_ref, *refs):
    x_refs, (y_ref, keep_ref, send_ref, both_ref) = refs[:-4], refs[-4:]
    side, column = place_ref[0], place_ref[1]
    mode_count = x_refs[0].shape[1]
    chunk_rows = y_ref.shape[2]
    per_device = mode_count // (columns * cores)
    piece = chunk_rows // (columns * cores)
    band = cores * per_device
    contract_last = (((1,), (1,)), ((), ()))
    for slot, (x, chunk, spec) in enumerate(steps):
        x_ref = x_refs[x]
        y = y_ref[chunk].reshape(2 * chunk_rows, y_ref.shape[3])
        y = (y.astype(jnp.float32) * spec_ref[pl.ds(spec, 1), :]).astype(jnp.bfloat16)
        for e in range(columns):
            rows = pl.ds(e * band, band)
            z0 = lax.dot_general(
                x_ref[0, rows, :], y, contract_last, preferred_element_type=jnp.float32
            )
            z1 = lax.dot_general(
                x_ref[1, rows, :], y, contract_last, preferred_element_type=jnp.float32
            )
            real = z0[:, :chunk_rows] + z1[:, chunk_rows:]
            imag = z1[:, :chunk_rows] - z0[:, chunk_rows:]

            @pl.when(side == DOWN)
            def _():
                for c in range(cores):
                    own = slice(c * per_device, (c + 1) * per_device)
                    both_ref[e, slot, c, 0] = real[own].astype(jnp.bfloat16)
                    both_ref[e, slot, c, 1] = imag[own].astype(jnp.bfloat16)

            @pl.when(side == UP)
            def _():
                for part, value in ((0, real), (1, -imag)):
                    for b in range(band // LANES):
                        block = value[b * LANES : (b + 1) * LANES].T.astype(jnp.bfloat16)
                        at = (e * (band // LANES) + b) * piece
                        for d in range(columns * cores):
                            both_ref[d // cores, slot, d % cores, part, at : at + piece] = block[
                                d * piece : (d + 1) * piece
                            ]

    keep_ref[...] = both_ref[column]
    send_ref[...] = both_ref[1 - column]


def products(steps, place, specs, xs, y, columns, cores):
    mode_count = xs[0].shape[1]
    chunk_rows = y.shape[2]
    held = (len(steps), cores, 2, mode_count // (columns * cores), chunk_rows)
    width = y.shape[3]
    flops = len(steps) * 8 * mode_count * chunk_rows * width
    vmem = pl.BlockSpec(memory_space=pltpu.VMEM)

    def body(*refs):
        products_body(steps, columns, cores, *refs)

    return pl.pallas_call(
        body,
        out_shape=[jax.ShapeDtypeStruct(held, jnp.bfloat16)] * 2,
        in_specs=[pl.BlockSpec(memory_space=pltpu.SMEM)] + [vmem] * (len(xs) + 2),
        out_specs=[vmem, vmem],
        scratch_shapes=[pltpu.VMEM((columns,) + held, jnp.bfloat16)],
        compiler_params=pltpu.CompilerParams(vmem_limit_bytes=32 * 2**20),
        cost_estimate=pl.CostEstimate(
            flops=flops, bytes_accessed=2 * width * 2 * (len(xs) * mode_count), transcendentals=0
        ),
    )(place, specs, *xs, y)


def meet_in_the_middle(beam_matrix, sky_spectrum, taper_tiles, noise_tiles):
    columns, cores = lax.axis_size("ell"), lax.axis_size("pol")
    freqs = lax.axis_size("freq")
    freq, column, side = (lax.axis_index(name) for name in ("freq", "ell", "pol"))
    own = beam_matrix[0]
    mode_count, width = own.shape[1], own.shape[2]
    sharers = columns * cores
    per_device = mode_count // sharers
    chunks = mode_count // LANES
    piece = LANES // sharers
    down = side == DOWN
    place = jnp.stack([side, column]).astype(jnp.int32)

    def along(block, route):
        pairs = [(f * cores + p, g * cores + q) for (f, p), (g, q) in route]
        return lax.ppermute(block, ("freq", "pol"), pairs)

    def over_columns(block, members):
        pairs = [
            ((f * columns + e) * cores + p, (f * columns + 1 - e) * cores + p)
            for f, p in members
            for e in range(columns)
        ]
        return lax.ppermute(block, ("freq", "ell", "pol"), pairs)

    def other_core(block):
        return lax.ppermute(block, "pol", [(0, 1), (1, 0)])

    def chunk_of(k):
        straight = own[:, k * LANES : (k + 1) * LANES]
        spread = own.reshape(2, sharers, per_device, width)[:, :, k * piece : (k + 1) * piece]
        return jnp.where(down, straight, spread.reshape(2, LANES, width))

    middle = [(LOW, DOWN), (HIGH, UP)]
    first, last = 0, freqs - 1

    below = lax.ppermute(sky_spectrum[0], "freq", [(f, f + 1) for f in range(freqs - 1)])
    below2 = lax.ppermute(sky_spectrum[0], "freq", [(f, f + 2) for f in range(freqs - 2)])

    outer = along(
        own,
        [
            ((first, DOWN), (LOW, DOWN)),
            ((last, UP), (HIGH, UP)),
            ((LOW, UP), (first, UP)),
            ((HIGH, DOWN), (last, DOWN)),
        ],
    )
    own_chunks = [chunk_of(k) for k in range(chunks)]
    near = [
        along(c, [((HIGH, DOWN), (LOW, DOWN)), ((LOW, UP), (HIGH, UP))]) for c in own_chunks
    ]
    far_chunks, outer = lax.optimization_barrier((own_chunks, outer))
    far = [
        along(c, [((last, DOWN), (LOW, DOWN)), ((first, UP), (HIGH, UP))]) for c in far_chunks
    ]

    own_sky = sky_spectrum[0]
    near_spec = jnp.where(
        down, jnp.stack([below[1], own_sky[0]]), jnp.stack([below[1], below[0]])
    )
    far_spec = jnp.where(
        down, jnp.stack([below[2], own_sky[1]]), jnp.stack([below2[2], below2[1]])
    )
    end_spec = jnp.where(down, below[:1], own_sky[:1])

    def summed(kept, sent, members):
        arrived = over_columns(sent, members)
        return (kept.astype(jnp.float32) + arrived.astype(jnp.float32)).astype(jnp.bfloat16)

    def pair(y, specs):
        steps = [(0, 0, 0), (1, 0, 1)]
        return products(steps, place, specs, [outer, own], y[None], columns, cores)

    end_steps = [(0, k, 0) for k in range(chunks)]
    end_sum = summed(
        *products(end_steps, place, end_spec, [outer], jnp.stack(own_chunks), columns, cores),
        middle + [(first, UP), (last, DOWN)],
    )
    end_back = along(end_sum, [((LOW, DOWN), (first, DOWN)), ((last, DOWN), (HIGH, DOWN))])
    end_home = jnp.where(down, end_back, end_sum)

    at_low = (freq == LOW) & down
    near_home, far_home = [], []
    for block in near:
        total = summed(*pair(block, near_spec), middle)
        back = along(total, [((LOW, DOWN), (first, DOWN)), ((HIGH, UP), (LOW, UP))])
        near_home.append(jnp.where(at_low, total, back))
    for block in far:
        total = summed(*pair(block, far_spec), middle)
        back = along(total, [((LOW, DOWN), (first, DOWN)), ((HIGH, UP), (first, UP))])
        far_home.append(jnp.where(at_low, total, back))

    def exchanged(home):
        kept = lax.dynamic_index_in_dim(home, side, 1, keepdims=False)
        arrived = other_core(lax.dynamic_index_in_dim(home, 1 - side, 1, keepdims=False))
        return jnp.where(down, kept, arrived), jnp.where(down, arrived, kept)

    def straight_tile(parts):
        return jnp.stack(parts).transpose(2, 1, 0, 3).reshape(per_device, 2, mode_count)

    def spread_tile(parts):
        stacked = jnp.stack(parts).reshape(chunks, 2, mode_count // LANES, piece, LANES)
        return stacked.transpose(0, 3, 1, 2, 4).reshape(per_device, 2, mode_count)

    end_d, end_u = exchanged(end_home)
    near_d, near_u = zip(*[exchanged(h) for h in near_home])
    far_d, far_u = zip(*[exchanged(h) for h in far_home])
    zero = jnp.zeros((per_device, 2, mode_count), jnp.float32)

    def total_of(d_parts, u_parts):
        return straight_tile(d_parts).astype(jnp.float32) + spread_tile(u_parts).astype(
            jnp.float32
        )

    end_tile = total_of([end_d[k] for k in range(chunks)], [end_u[k] for k in range(chunks)])
    at_first, at_lower = freq == first, freq == LOW
    sum0 = jnp.where(
        at_lower,
        total_of([c[1] for c in near_d], [c[1] for c in near_u]),
        jnp.where(freq == last, zero, end_tile),
    )
    sum1 = jnp.where(
        at_first,
        total_of([c[0] for c in near_d], [c[1] for c in far_u]),
        jnp.where(at_lower, total_of([c[1] for c in far_d], [c[0] for c in near_u]), zero),
    )
    sum2 = jnp.where(at_first, total_of([c[0] for c in far_d], [c[0] for c in far_u]), zero)
    tiles = jnp.stack([sum0, sum1, sum2])
    taper = taper_tiles.astype(jnp.float32)[:, :, None, :]
    return (taper * tiles + noise_tiles[0].astype(jnp.float32))[None]


def local(beam_matrix, sky_spectrum, taper_tiles, noise_tiles):
    freqs, columns, cores = (lax.axis_size(name) for name in ("freq", "ell", "pol"))
    separations = sky_spectrum.shape[1]
    mode_count = beam_matrix.shape[2]
    two_below_two_above = freqs == 2 * HIGH and separations == freqs - 1
    halves = columns == 2 and cores == 2
    whole_pieces = mode_count % (LANES * columns * cores) == 0
    if two_below_two_above and halves and whole_pieces:
        return meet_in_the_middle(beam_matrix, sky_spectrum, taper_tiles, noise_tiles)
    return partners_passed_down(beam_matrix, sky_spectrum, taper_tiles, noise_tiles)


def solution(mesh):
    placed = (
        P(("grp", "freq"), None, None, ("ell", "pol")),
        P(("grp", "freq"), None, ("ell", "pol")),
        P(None, ("ell", "pol"), None),
        P(("grp", "freq"), None, ("ell", "pol"), None, None),
    )
    return jax.shard_map(
        local,
        mesh=mesh,
        in_specs=placed,
        out_specs=P(("grp", "freq"), None, ("ell", "pol"), None, None),
        check_vma=False,
    )
```

time: 443 us -> 256 us (0.58)
  waiting for transfers between devices: 380 us -> 89.3 us
  Pallas kernels: 0 us -> 51.7 us
  starting transfers between devices: 4.13 us -> 42 us
  local copies, waits for them, and re-layouts: 14 us -> 47.4 us
  matrix products: 16.5 us -> 0 us
  between operations: 13.3 us -> 1.01 us
  other arithmetic: 14 us -> 22.9 us
    ppermute x3 -> x38, waiting for transfers between devices: 341 us -> 89.3 us  [the longest x18 60.5 us: along(): return lax.ppermute(block, ('freq', 'pol'), pairs)]
    pallas_call x0 -> x9, Pallas kernels: none -> 51.7 us  [products(): pl.pallas_call(body, out_shape=[jax.ShapeDtypeStruct(held, jnp.bfloat16)]...]
    reduce_scatter x3 -> x0, waiting for transfers between devices: 39 us -> none  [local(): lax.psum_scatter(tile_term(jnp.int32(0), lax.axis_size(('ell', 'pol')) *...]
    ppermute x3 -> x38, starting transfers between devices: 3.86 us -> 42 us  [the longest x18 25.2 us: along(): return lax.ppermute(block, ('freq', 'pol'), pairs)]
    convert_element_type x0 -> x21, local copies, waits for them, and re-layouts: none -> 32.4 us  [the longest x15 22.9 us: total_of(): spread_tile(u_parts).astype(jnp.float32)]
    dot_general x3 -> x0, matrix products: 16.5 us -> none  [tile_term(): lax.dot_general(left_rows, stacked_right, (((1,), (1,)), ((), ())), prefe...]
    squeeze x5 -> x9, local copies, waits for them, and re-layouts: 9.66 us -> 0.17 us  [exchanged(): lax.dynamic_index_in_dim(home, 1 - side, 1, keepdims=False)]
    unnamed x8 -> x32, local copies, waits for them, and re-layouts: 1.28 us -> 9.98 us
  transfers between devices with their start and end apart: 6 -> 38, of which waited for: 4 -> 14; matrix products, arithmetic and copies ran while one was open for 9% -> 19% of each run, Pallas kernels for 0% -> 20%
where the time goes in v1:
time: 256 us; the launch traced here: 254 us
  waiting for transfers between devices  89.3 us (35%)
  Pallas kernels  51.7 us (20%)
  local copies, waits for them, and re-layouts  47.4 us (19%)
  starting transfers between devices  42 us (16%)
  other arithmetic  22.9 us (9%)
    ppermute x18, waiting for transfers between devices, along(): return lax.ppermute(block, ('freq', 'pol'), pairs)  60.5 us
    pallas_call x9, Pallas kernels, products(): pl.pallas_call(body, out_shape=[jax.ShapeDtypeStruct(held, jnp.bfloat16)]...  51.7 us
    ppermute x18, starting transfers between devices, along(): return lax.ppermute(block, ('freq', 'pol'), pairs)  25.2 us
    ppermute x1, waiting for transfers between devices, meet_in_the_middle(): lax.ppermute(sky_spectrum[0], 'freq', [(f, f + 1) for f in range(freqs -...  22.9 us
    convert_element_type x15, local copies, waits for them, and re-layouts, total_of(): spread_tile(u_parts).astype(jnp.float32)  22.9 us
    unnamed x32, local copies, waits for them, and re-layouts  9.98 us
    ppermute x9, starting transfers between devices, over_columns(): return lax.ppermute(block, ('freq', 'ell', 'pol'), pairs)  9.2 us
    convert_element_type x5, local copies, waits for them, and re-layouts, total_of(): straight_tile(d_parts).astype(jnp.float32)  7.4 us
  transfers between devices with their start and end apart: 38, of which 14 were waited for; matrix products, arithmetic and copies ran while one was open for 19% of the time, Pallas kernels for 20%

profile of v1, /device:TPU:0, one launch (start us, length us, event | category | flops | bytes accessed | tf_op | source)
XLA Modules:
  0.0 254.3 jit_solution(7221410956109221059)
XLA Ops:
  0.0 6.9 %collective-permute-start.1 = (bf16[2,512,2048]{2,1,0:T(8,128)(2,1)}, bf16[2,512,2048]{2,1,0:T(8,128)(2,1)}, u32[]{:S(2)}, u32[]{:S(2)}) collective-permute-start(bf16[2,512,2048]{2,1,0:T(8,128)(2,1)} %bitcast.147), channel_id=1, source_target_pairs={{0,4},{13,9},{5,1},{8,12},{2,6},{15,11},{7,3},{10,14},{16,20},{29,... | collective-permute-start | bytes 12582920 | tf_op jit(solution)/shard_map/ppermute | solution.py:131
  9.0 5.1 %collective-permute-start.21 = (f32[3,2048]{1,0:T(4,128)S(1)}, f32[3,2048]{1,0:T(4,128)S(1)}, u32[]{:S(2)}, u32[]{:S(2)}) collective-permute-start(f32[3,2048]{1,0:T(4,128)S(1)} %bitcast.174), channel_id=1, source_target_pairs={{0,8},{4,12},{1,9},{5,13},{2,10},{6,14},{3,11},{7,15},{16,24},{20,... | collective-permute-start | bytes 73736 | tf_op jit(solution)/shard_map/ppermute | solution.py:153
  14.1 2.6 %fusion.7 = (bf16[2,4,32,2048]{3,2,1,0:T(8,128)(2,1)S(1)}, bf16[2,4,32,2048]{3,2,1,0:T(8,128)(2,1)S(1)}, bf16[2,4,32,2048]{3,2,1,0:T(8,128)(2,1)S(1)}, bf16[2,4,32,2048]{3,2,1,0:T(8,128)(2,1)S(1)}) fusion(bf16[2,4,128,2048]{3,2,1,0:T(8,128)(2,1)} %bitcast.148), kind=kLoop, calls=%fused_computation.85 | loop fusion | bytes 8388608 | tf_op jit(solution)/shard_map/slice | solution.py:146
  17.6 2.5 slice_select_fusion
  21.5 3.8 %pad_maximum_fusion.refs_3_ = bf16[4,2,128,2048]{3,2,1,0:T(8,128)(2,1)} fusion(bf16[1,2,128,2048]{3,2,1,0:T(8,128)(2,1)} %bitcast.28, bf16[1,2,128,2048]{3,2,1,0:T(8,128)(2,1)} %bitcast.27, bf16[1,2,128,2048]{3,2,1,0:T(8,128)(2,1)} %bitcast.26, bf16[1,2,128,2048]{3,2,1,0:T(8,128)(2,1)} %bitcast.25), kind=kLoop, calls=%fused_computation | loop fusion | flops 6291456 | bytes 8388608 | tf_op jit(solution)/shard_map/stack | solution.py:192
  27.2 2.1 copy.38
  29.3 22.9 %collective-permute-done = f32[3,2048]{1,0:T(4,128)S(1)} collective-permute-done((f32[3,2048]{1,0:T(4,128)S(1)}, f32[3,2048]{1,0:T(4,128)S(1)}, u32[]{:S(2)}, u32[]{:S(2)}) %collective-permute-start) | collective-permute-done | bytes 24608 | tf_op jit(solution)/shard_map/ppermute | solution.py:152
  56.3 2.2 copy-done.1
  59.7 5.2 %shard_map.49 = (bf16[2,2,2,128,128]{4,3,2,1,0:T(8,128)(2,1)S(1)}, bf16[2,2,2,128,128]{4,3,2,1,0:T(8,128)(2,1)S(1)}) custom-call(s32[2]{0:T(128)S(1)} %pad_add_fusion.refs_0_, f32[2,2048]{1,0:T(2,128)S(1)} %fusion.6.refs_1_, bf16[2,512,2048]{2,1,0:T(8,128)(2,1)} %collective-permute-done.1.refs_2_, bf16[2,512,2048]{2,1,0:T(8,128)(2,1)S(1)} %bitcast.150, ...), custom_call_target="tpu_custom_call" | custom-call | flops 2147483648 | bytes 8388608 | tf_op jit(solution)/shard_map/pallas_call | solution.py:103
  65.7 5.4 %shard_map.48 = (bf16[2,2,2,128,128]{4,3,2,1,0:T(8,128)(2,1)S(1)}, bf16[2,2,2,128,128]{4,3,2,1,0:T(8,128)(2,1)S(1)}) custom-call(s32[2]{0:T(128)S(1)} %pad_add_fusion.refs_0_, f32[2,2048]{1,0:T(2,128)S(1)} %fusion.6.refs_1_, bf16[2,512,2048]{2,1,0:T(8,128)(2,1)} %collective-permute-done.1.refs_2_, bf16[2,512,2048]{2,1,0:T(8,128)(2,1)S(1)} %bitcast.151, ...), custom_call_target="tpu_custom_call" | custom-call | flops 2147483648 | bytes 8388608 | tf_op jit(solution)/shard_map/pallas_call | solution.py:103
  71.1 8.4 %shard_map.50 = (bf16[4,2,2,128,128]{4,3,2,1,0:T(8,128)(2,1)S(1)}, bf16[4,2,2,128,128]{4,3,2,1,0:T(8,128)(2,1)S(1)}) custom-call(s32[2]{0:T(128)S(1)} %pad_add_fusion.refs_0_, f32[1,2048]{1,0:T(1,128)S(1)} %get-tuple-element.109.refs_1_, bf16[2,512,2048]{2,1,0:T(8,128)(2,1)} %collective-permute-done.1.refs_2_, bf16[4,2,128,2048]{3,2,1,0:T(8,128)(2,1)S(1)} %copy-done.4), custom_call_target="tpu_custom_call" | custom-call | flops 4294967296 | bytes 4194304 | tf_op jit(solution)/shard_map/pallas_call | solution.py:103
  80.4 5.2 %shard_map.47 = (bf16[2,2,2,128,128]{4,3,2,1,0:T(8,128)(2,1)S(1)}, bf16[2,2,2,128,128]{4,3,2,1,0:T(8,128)(2,1)S(1)}) custom-call(s32[2]{0:T(128)S(1)} %pad_add_fusion.refs_0_, f32[2,2048]{1,0:T(2,128)S(1)} %fusion.6.refs_1_, bf16[2,512,2048]{2,1,0:T(8,128)(2,1)} %collective-permute-done.1.refs_2_, bf16[2,512,2048]{2,1,0:T(8,128)(2,1)S(1)} %bitcast.152, ...), custom_call_target="tpu_custom_call" | custom-call | flops 2147483648 | bytes 8388608 | tf_op jit(solution)/shard_map/pallas_call | solution.py:103
  86.4 5.2 %shard_map.46 = (bf16[2,2,2,128,128]{4,3,2,1,0:T(8,128)(2,1)S(1)}, bf16[2,2,2,128,128]{4,3,2,1,0:T(8,128)(2,1)S(1)}) custom-call(s32[2]{0:T(128)S(1)} %pad_add_fusion.refs_0_, f32[2,2048]{1,0:T(2,128)S(1)} %fusion.6.refs_1_, bf16[2,512,2048]{2,1,0:T(8,128)(2,1)} %collective-permute-done.1.refs_2_, bf16[2,512,2048]{2,1,0:T(8,128)(2,1)S(1)} %bitcast.153, ...), custom_call_target="tpu_custom_call" | custom-call | flops 2147483648 | bytes 8388608 | tf_op jit(solution)/shard_map/pallas_call | solution.py:103
  97.7 30.1 %collective-permute-done.16 = bf16[2,2,2,128,128]{4,3,2,1,0:T(8,128)(2,1)S(1)} collective-permute-done((bf16[2,2,2,128,128]{4,3,2,1,0:T(8,128)(2,1)S(1)}, bf16[2,2,2,128,128]{4,3,2,1,0:T(8,128)(2,1)S(1)}, u32[]{:S(2)}, u32[]{:S(2)}) %collective-permute-start.16) | collective-permute-done | bytes 262176 | tf_op jit(solution)/shard_map/ppermute | solution.py:131
  129.1 4.3 %collective-permute-done.12 = bf16[2,2,2,128,128]{4,3,2,1,0:T(8,128)(2,1)S(1)} collective-permute-done((bf16[2,2,2,128,128]{4,3,2,1,0:T(8,128)(2,1)S(1)}, bf16[2,2,2,128,128]{4,3,2,1,0:T(8,128)(2,1)S(1)}, u32[]{:S(2)}, u32[]{:S(2)}) %collective-permute-start.12) | collective-permute-done | bytes 262176 | tf_op jit(solution)/shard_map/ppermute | solution.py:131
  137.9 3.7 %collective-permute-done.4 = bf16[2,2,2,128,128]{4,3,2,1,0:T(8,128)(2,1)S(1)} collective-permute-done((bf16[2,2,2,128,128]{4,3,2,1,0:T(8,128)(2,1)S(1)}, bf16[2,2,2,128,128]{4,3,2,1,0:T(8,128)(2,1)S(1)}, u32[]{:S(2)}, u32[]{:S(2)}) %collective-permute-start.4) | collective-permute-done | bytes 262176 | tf_op jit(solution)/shard_map/ppermute | solution.py:131
  152.4 2.1 reshape.285
  154.5 2.1 copy.50
  158.6 2.2 copy.40
  160.8 2.1 reshape.279
  164.9 2.1 copy.39
  168.5 2.2 copy-done.3
  170.7 6.0 %shard_map.54 = (bf16[2,2,2,128,128]{4,3,2,1,0:T(8,128)(2,1)S(1)}, bf16[2,2,2,128,128]{4,3,2,1,0:T(8,128)(2,1)}) custom-call(s32[2]{0:T(128)S(1)} %pad_add_fusion.refs_0_, f32[2,2048]{1,0:T(2,128)S(1)} %maximum_select_fusion.refs_1_, bf16[2,512,2048]{2,1,0:T(8,128)(2,1)} %collective-permute-done.1.refs_2_, bf16[2,512,2048]{2,1,0:T(8,128)(2,1)S(1)} %bitcast.154, ...), custom_call_target="tpu_custom_call" | custom-call | flops 2147483648 | bytes 8388608 | tf_op jit(solution)/shard_map/pallas_call | solution.py:103
  178.0 5.5 %shard_map.53 = (bf16[2,2,2,128,128]{4,3,2,1,0:T(8,128)(2,1)S(1)}, bf16[2,2,2,128,128]{4,3,2,1,0:T(8,128)(2,1)S(1)}) custom-call(s32[2]{0:T(128)S(1)} %pad_add_fusion.refs_0_, f32[2,2048]{1,0:T(2,128)S(1)} %maximum_select_fusion.refs_1_, bf16[2,512,2048]{2,1,0:T(8,128)(2,1)} %collective-permute-done.1.refs_2_, bf16[2,512,2048]{2,1,0:T(8,128)(2,1)S(1)} %bitcast.155, ...), custom_call_target="tpu_custom_call" | custom-call | flops 2147483648 | bytes 8388608 | tf_op jit(solution)/shard_map/pallas_call | solution.py:103
  184.9 5.2 %shard_map.52 = (bf16[2,2,2,128,128]{4,3,2,1,0:T(8,128)(2,1)S(1)}, bf16[2,2,2,128,128]{4,3,2,1,0:T(8,128)(2,1)S(1)}) custom-call(s32[2]{0:T(128)S(1)} %pad_add_fusion.refs_0_, f32[2,2048]{1,0:T(2,128)S(1)} %maximum_select_fusion.refs_1_, bf16[2,512,2048]{2,1,0:T(8,128)(2,1)} %collective-permute-done.1.refs_2_, bf16[2,512,2048]{2,1,0:T(8,128)(2,1)S(1)} %bitcast.156, ...), custom_call_target="tpu_custom_call" | custom-call | flops 2147483648 | bytes 8388608 | tf_op jit(solution)/shard_map/pallas_call | solution.py:103
  191.5 5.5 %shard_map.51 = (bf16[2,2,2,128,128]{4,3,2,1,0:T(8,128)(2,1)S(1)}, bf16[2,2,2,128,128]{4,3,2,1,0:T(8,128)(2,1)S(1)}) custom-call(s32[2]{0:T(128)S(1)} %pad_add_fusion.refs_0_, f32[2,2048]{1,0:T(2,128)S(1)} %maximum_select_fusion.refs_1_, bf16[2,512,2048]{2,1,0:T(8,128)(2,1)} %collective-permute-done.1.refs_2_, bf16[2,512,2048]{2,1,0:T(8,128)(2,1)S(1)} %bitcast.157, ...), custom_call_target="tpu_custom_call" | custom-call | flops 2147483648 | bytes 8388608 | tf_op jit(solution)/shard_map/pallas_call | solution.py:103
  200.6 2.1 reshape.281
  217.3 12.8 %collective-permute-done.36 = bf16[2,2,2,128,128]{4,3,2,1,0:T(8,128)(2,1)S(1)} collective-permute-done((bf16[2,2,2,128,128]{4,3,2,1,0:T(8,128)(2,1)S(1)}, bf16[2,2,2,128,128]{4,3,2,1,0:T(8,128)(2,1)S(1)}, u32[]{:S(2)}, u32[]{:S(2)}) %collective-permute-start.36) | collective-permute-done | bytes 262176 | tf_op jit(solution)/shard_map/ppermute | solution.py:131
  230.3 2.7 %collective-permute-done.32 = bf16[2,2,2,128,128]{4,3,2,1,0:T(8,128)(2,1)S(1)} collective-permute-done((bf16[2,2,2,128,128]{4,3,2,1,0:T(8,128)(2,1)S(1)}, bf16[2,2,2,128,128]{4,3,2,1,0:T(8,128)(2,1)S(1)}, u32[]{:S(2)}, u32[]{:S(2)}) %collective-permute-start.32) | collective-permute-done | bytes 262176 | tf_op jit(solution)/shard_map/ppermute | solution.py:131
  233.1 2.7 %collective-permute-done.28 = bf16[2,2,2,128,128]{4,3,2,1,0:T(8,128)(2,1)S(1)} collective-permute-done((bf16[2,2,2,128,128]{4,3,2,1,0:T(8,128)(2,1)S(1)}, bf16[2,2,2,128,128]{4,3,2,1,0:T(8,128)(2,1)S(1)}, u32[]{:S(2)}, u32[]{:S(2)}) %collective-permute-start.28) | collective-permute-done | bytes 262176 | tf_op jit(solution)/shard_map/ppermute | solution.py:131
  235.9 2.7 %collective-permute-done.24 = bf16[2,2,2,128,128]{4,3,2,1,0:T(8,128)(2,1)S(1)} collective-permute-done((bf16[2,2,2,128,128]{4,3,2,1,0:T(8,128)(2,1)S(1)}, bf16[2,2,2,128,128]{4,3,2,1,0:T(8,128)(2,1)S(1)}, u32[]{:S(2)}, u32[]{:S(2)}) %collective-permute-start.24) | collective-permute-done | bytes 262176 | tf_op jit(solution)/shard_map/ppermute | solution.py:131
  252.2 2.1 copy.55
  (177 shorter events, 77.5 us)
Async XLA Ops:
  0.0 53.8 %collective-permute-start.1 = (bf16[2,512,2048]{2,1,0:T(8,128)(2,1)}, bf16[2,512,2048]{2,1,0:T(8,128)(2,1)}, u32[]{:S(2)}, u32[]{:S(2)}) collective-permute-start(bf16[2,512,2048]{2,1,0:T(8,128)(2,1)} %bitcast.147), channel_id=1, source_target_pairs={{0,4},{13,9},{5,1},{8,12},{2,6},{15,11},{7,3},{10,14},{16,20},{29,... | collective-permute-start | bytes 12582920 | tf_op jit(solution)/shard_map/ppermute | solution.py:131
  7.7 44.5 %collective-permute-start = (f32[3,2048]{1,0:T(4,128)S(1)}, f32[3,2048]{1,0:T(4,128)S(1)}, u32[]{:S(2)}, u32[]{:S(2)}) collective-permute-start(f32[3,2048]{1,0:T(4,128)S(1)} %bitcast.173), channel_id=1, source_target_pairs={{0,4},{4,8},{8,12},{1,5},{5,9},{9,13},{2,6},{6,10},{10,14},{3,7},{... | collective-permute-start | bytes 73736 | tf_op jit(solution)/shard_map/ppermute | solution.py:152
  9.0 44.0 %collective-permute-start.21 = (f32[3,2048]{1,0:T(4,128)S(1)}, f32[3,2048]{1,0:T(4,128)S(1)}, u32[]{:S(2)}, u32[]{:S(2)}) collective-permute-start(f32[3,2048]{1,0:T(4,128)S(1)} %bitcast.174), channel_id=1, source_target_pairs={{0,8},{4,12},{1,9},{5,13},{2,10},{6,14},{3,11},{7,15},{16,24},{20,... | collective-permute-start | bytes 73736 | tf_op jit(solution)/shard_map/ppermute | solution.py:153
  20.0 34.5 %collective-permute-start.14 = (bf16[2,128,2048]{2,1,0:T(8,128)(2,1)}, bf16[2,128,2048]{2,1,0:T(8,128)(2,1)S(1)}, u32[]{:S(2)}, u32[]{:S(2)}) collective-permute-start(bf16[2,128,2048]{2,1,0:T(8,128)(2,1)} %get-tuple-element.48), channel_id=1, source_target_pairs={{8,4},{5,9},{10,6},{7,11},{24,20},{21,25},{26,22},{23,27}} | collective-permute-start | bytes 3145736 | tf_op jit(solution)/shard_map/ppermute | solution.py:131
  20.7 44.2 %collective-permute-start.10 = (bf16[2,128,2048]{2,1,0:T(8,128)(2,1)}, bf16[2,128,2048]{2,1,0:T(8,128)(2,1)S(1)}, u32[]{:S(2)}, u32[]{:S(2)}) collective-permute-start(bf16[2,128,2048]{2,1,0:T(8,128)(2,1)} %get-tuple-element.45), channel_id=1, source_target_pairs={{8,4},{5,9},{10,6},{7,11},{24,20},{21,25},{26,22},{23,27}} | collective-permute-start | bytes 3145736 | tf_op jit(solution)/shard_map/ppermute | solution.py:131
  52.2 27.4 %collective-permute-start.6 = (bf16[2,128,2048]{2,1,0:T(8,128)(2,1)}, bf16[2,128,2048]{2,1,0:T(8,128)(2,1)S(1)}, u32[]{:S(2)}, u32[]{:S(2)}) collective-permute-start(bf16[2,128,2048]{2,1,0:T(8,128)(2,1)} %get-tuple-element.42), channel_id=1, source_target_pairs={{8,4},{5,9},{10,6},{7,11},{24,20},{21,25},{26,22},{23,27}} | collective-permute-start | bytes 3145736 | tf_op jit(solution)/shard_map/ppermute | solution.py:131
  53.0 32.7 %collective-permute-start.2 = (bf16[2,128,2048]{2,1,0:T(8,128)(2,1)}, bf16[2,128,2048]{2,1,0:T(8,128)(2,1)S(1)}, u32[]{:S(2)}, u32[]{:S(2)}) collective-permute-start(bf16[2,128,2048]{2,1,0:T(8,128)(2,1)} %get-tuple-element.39), channel_id=1, source_target_pairs={{8,4},{5,9},{10,6},{7,11},{24,20},{21,25},{26,22},{23,27}} | collective-permute-start | bytes 3145736 | tf_op jit(solution)/shard_map/ppermute | solution.py:131
  53.8 114.7 %collective-permute-start.34 = (bf16[2,128,2048]{2,1,0:T(8,128)(2,1)}, bf16[2,128,2048]{2,1,0:T(8,128)(2,1)S(1)}, u32[]{:S(2)}, u32[]{:S(2)}) collective-permute-start(bf16[2,128,2048]{2,1,0:T(8,128)(2,1)} %get-tuple-element.48), channel_id=1, source_target_pairs={{12,4},{1,9},{14,6},{3,11},{28,20},{17,25},{30,22},{19,27}} | collective-permute-start | bytes 3145736 | tf_op jit(solution)/shard_map/ppermute | solution.py:131
  55.6 122.4 %collective-permute-start.30 = (bf16[2,128,2048]{2,1,0:T(8,128)(2,1)}, bf16[2,128,2048]{2,1,0:T(8,128)(2,1)S(1)}, u32[]{:S(2)}, u32[]{:S(2)}) collective-permute-start(bf16[2,128,2048]{2,1,0:T(8,128)(2,1)} %get-tuple-element.45), channel_id=1, source_target_pairs={{12,4},{1,9},{14,6},{3,11},{28,20},{17,25},{30,22},{19,27}} | collective-permute-start | bytes 3145736 | tf_op jit(solution)/shard_map/ppermute | solution.py:131
  65.0 26.6 %collective-permute-start.15 = (bf16[2,2,2,128,128]{4,3,2,1,0:T(8,128)(2,1)S(1)}, bf16[2,2,2,128,128]{4,3,2,1,0:T(8,128)(2,1)S(1)}, u32[]{:S(2)}, u32[]{:S(2)}) collective-permute-start(bf16[2,2,2,128,128]{4,3,2,1,0:T(8,128)(2,1)S(1)} %get-tuple-element.36), channel_id=1, source_target_pairs={{4,6},{6,4},{9,11},{11,9},{20,22},{22,20},{25,27},{27,25}} | collective-permute-start | bytes 786440 | tf_op jit(solution)/shard_map/ppermute | solution.py:139
  79.6 12.8 %collective-permute-start.11 = (bf16[2,2,2,128,128]{4,3,2,1,0:T(8,128)(2,1)S(1)}, bf16[2,2,2,128,128]{4,3,2,1,0:T(8,128)(2,1)S(1)}, u32[]{:S(2)}, u32[]{:S(2)}) collective-permute-start(bf16[2,2,2,128,128]{4,3,2,1,0:T(8,128)(2,1)S(1)} %get-tuple-element.34), channel_id=1, source_target_pairs={{4,6},{6,4},{9,11},{11,9},{20,22},{22,20},{25,27},{27,25}} | collective-permute-start | bytes 786440 | tf_op jit(solution)/shard_map/ppermute | solution.py:139
  85.7 7.5 %collective-permute-start.7 = (bf16[2,2,2,128,128]{4,3,2,1,0:T(8,128)(2,1)S(1)}, bf16[2,2,2,128,128]{4,3,2,1,0:T(8,128)(2,1)S(1)}, u32[]{:S(2)}, u32[]{:S(2)}) collective-permute-start(bf16[2,2,2,128,128]{4,3,2,1,0:T(8,128)(2,1)S(1)} %get-tuple-element.32), channel_id=1, source_target_pairs={{4,6},{6,4},{9,11},{11,9},{20,22},{22,20},{25,27},{27,25}} | collective-permute-start | bytes 786440 | tf_op jit(solution)/shard_map/ppermute | solution.py:139
  92.4 3.0 %collective-permute-start.18 = (bf16[4,2,2,128,128]{4,3,2,1,0:T(8,128)(2,1)S(1)}, bf16[4,2,2,128,128]{4,3,2,1,0:T(8,128)(2,1)S(1)}, u32[]{:S(2)}, u32[]{:S(2)}) collective-permute-start(bf16[4,2,2,128,128]{4,3,2,1,0:T(8,128)(2,1)S(1)} %get-tuple-element.38), channel_id=1, source_target_pairs={{4,6},{6,4},{9,11},{11,9},{1,3},{3,1},{12,14},{14,12},{20,22},{22,... | collective-permute-start | bytes 1572872 | tf_op jit(solution)/shard_map/ppermute | solution.py:139
  93.2 91.7 %collective-permute-start.26 = (bf16[2,128,2048]{2,1,0:T(8,128)(2,1)}, bf16[2,128,2048]{2,1,0:T(8,128)(2,1)S(1)}, u32[]{:S(2)}, u32[]{:S(2)}) collective-permute-start(bf16[2,128,2048]{2,1,0:T(8,128)(2,1)} %get-tuple-element.42), channel_id=1, source_target_pairs={{12,4},{1,9},{14,6},{3,11},{28,20},{17,25},{30,22},{19,27}} | collective-permute-start | bytes 3145736 | tf_op jit(solution)/shard_map/ppermute | solution.py:131
  94.0 33.8 %collective-permute-start.16 = (bf16[2,2,2,128,128]{4,3,2,1,0:T(8,128)(2,1)S(1)}, bf16[2,2,2,128,128]{4,3,2,1,0:T(8,128)(2,1)S(1)}, u32[]{:S(2)}, u32[]{:S(2)}) collective-permute-start(bf16[2,2,2,128,128]{4,3,2,1,0:T(8,128)(2,1)S(1)} %add_convert_fusion.5), channel_id=1, source_target_pairs={{4,0},{9,5},{6,2},{11,7},{20,16},{25,21},{22,18},{27,23}} | collective-permute-start | bytes 786440 | tf_op jit(solution)/shard_map/ppermute | solution.py:131
  95.4 38.0 %collective-permute-start.12 = (bf16[2,2,2,128,128]{4,3,2,1,0:T(8,128)(2,1)S(1)}, bf16[2,2,2,128,128]{4,3,2,1,0:T(8,128)(2,1)S(1)}, u32[]{:S(2)}, u32[]{:S(2)}) collective-permute-start(bf16[2,2,2,128,128]{4,3,2,1,0:T(8,128)(2,1)S(1)} %add_convert_fusion.6), channel_id=1, source_target_pairs={{4,0},{9,5},{6,2},{11,7},{20,16},{25,21},{22,18},{27,23}} | collective-permute-start | bytes 786440 | tf_op jit(solution)/shard_map/ppermute | solution.py:131
  127.8 8.4 %collective-permute-start.8 = (bf16[2,2,2,128,128]{4,3,2,1,0:T(8,128)(2,1)S(1)}, bf16[2,2,2,128,128]{4,3,2,1,0:T(8,128)(2,1)S(1)}, u32[]{:S(2)}, u32[]{:S(2)}) collective-permute-start(bf16[2,2,2,128,128]{4,3,2,1,0:T(8,128)(2,1)S(1)} %add_convert_fusion.7), channel_id=1, source_target_pairs={{4,0},{9,5},{6,2},{11,7},{20,16},{25,21},{22,18},{27,23}} | collective-permute-start | bytes 786440 | tf_op jit(solution)/shard_map/ppermute | solution.py:131
  133.4 8.3 %collective-permute-start.4 = (bf16[2,2,2,128,128]{4,3,2,1,0:T(8,128)(2,1)S(1)}, bf16[2,2,2,128,128]{4,3,2,1,0:T(8,128)(2,1)S(1)}, u32[]{:S(2)}, u32[]{:S(2)}) collective-permute-start(bf16[2,2,2,128,128]{4,3,2,1,0:T(8,128)(2,1)S(1)} %add_convert_fusion.8), channel_id=1, source_target_pairs={{4,0},{9,5},{6,2},{11,7},{20,16},{25,21},{22,18},{27,23}} | collective-permute-start | bytes 786440 | tf_op jit(solution)/shard_map/ppermute | solution.py:131
  136.2 55.3 %collective-permute-start.22 = (bf16[2,128,2048]{2,1,0:T(8,128)(2,1)}, bf16[2,128,2048]{2,1,0:T(8,128)(2,1)}, u32[]{:S(2)}, u32[]{:S(2)}) collective-permute-start(bf16[2,128,2048]{2,1,0:T(8,128)(2,1)} %get-tuple-element.39), channel_id=1, source_target_pairs={{12,4},{1,9},{14,6},{3,11},{28,20},{17,25},{30,22},{19,27}} | collective-permute-start | bytes 3145736 | tf_op jit(solution)/shard_map/ppermute | solution.py:131
  147.1 19.9 %collective-permute-start.19 = (bf16[4,2,2,128,128]{4,3,2,1,0:T(8,128)(2,1)}, bf16[4,2,2,128,128]{4,3,2,1,0:T(8,128)(2,1)}, u32[]{:S(2)}, u32[]{:S(2)}) collective-permute-start(bf16[4,2,2,128,128]{4,3,2,1,0:T(8,128)(2,1)} %add_convert_fusion), channel_id=1, source_target_pairs={{4,0},{12,8},{6,2},{14,10},{20,16},{28,24},{22,18},{30,26}} | collective-permute-start | bytes 1572872 | tf_op jit(solution)/shard_map/ppermute | solution.py:131
  168.1 30.4 %collective-permute-start.20 = (bf16[4,2,128,128]{3,2,1,0:T(8,128)(2,1)S(1)}, bf16[4,2,128,128]{3,2,1,0:T(8,128)(2,1)S(1)}, u32[]{:S(2)}, u32[]{:S(2)}) collective-permute-start(bf16[4,2,128,128]{3,2,1,0:T(8,128)(2,1)S(1)} %dynamic-slice_bitcast_fusion), channel_id=1, source_target_pairs={{0,1},{1,0},{2,3},{3,2},{4,5},{5,4},{6,7},{7,6},{8,9},{9,8},{10,11... | collective-permute-start | bytes 786440 | tf_op jit(solution)/shard_map/ppermute | solution.py:142
  176.7 31.3 %collective-permute-start.35 = (bf16[2,2,2,128,128]{4,3,2,1,0:T(8,128)(2,1)}, bf16[2,2,2,128,128]{4,3,2,1,0:T(8,128)(2,1)}, u32[]{:S(2)}, u32[]{:S(2)}) collective-permute-start(bf16[2,2,2,128,128]{4,3,2,1,0:T(8,128)(2,1)} %get-tuple-element.50), channel_id=1, source_target_pairs={{4,6},{6,4},{9,11},{11,9},{20,22},{22,20},{25,27},{27,25}} | collective-permute-start | bytes 786440 | tf_op jit(solution)/shard_map/ppermute | solution.py:139
  183.5 26.8 %collective-permute-start.31 = (bf16[2,2,2,128,128]{4,3,2,1,0:T(8,128)(2,1)S(1)}, bf16[2,2,2,128,128]{4,3,2,1,0:T(8,128)(2,1)}, u32[]{:S(2)}, u32[]{:S(2)}) collective-permute-start(bf16[2,2,2,128,128]{4,3,2,1,0:T(8,128)(2,1)S(1)} %get-tuple-element.47), channel_id=1, source_target_pairs={{4,6},{6,4},{9,11},{11,9},{20,22},{22,20},{25,27},{27,25}} | collective-permute-start | bytes 786440 | tf_op jit(solution)/shard_map/ppermute | solution.py:139
  190.1 22.5 %collective-permute-start.27 = (bf16[2,2,2,128,128]{4,3,2,1,0:T(8,128)(2,1)S(1)}, bf16[2,2,2,128,128]{4,3,2,1,0:T(8,128)(2,1)}, u32[]{:S(2)}, u32[]{:S(2)}) collective-permute-start(bf16[2,2,2,128,128]{4,3,2,1,0:T(8,128)(2,1)S(1)} %get-tuple-element.44), channel_id=1, source_target_pairs={{4,6},{6,4},{9,11},{11,9},{20,22},{22,20},{25,27},{27,25}} | collective-permute-start | bytes 786440 | tf_op jit(solution)/shard_map/ppermute | solution.py:139
  197.1 17.9 %collective-permute-start.23 = (bf16[2,2,2,128,128]{4,3,2,1,0:T(8,128)(2,1)S(1)}, bf16[2,2,2,128,128]{4,3,2,1,0:T(8,128)(2,1)}, u32[]{:S(2)}, u32[]{:S(2)}) collective-permute-start(bf16[2,2,2,128,128]{4,3,2,1,0:T(8,128)(2,1)S(1)} %get-tuple-element.41), channel_id=1, source_target_pairs={{4,6},{6,4},{9,11},{11,9},{20,22},{22,20},{25,27},{27,25}} | collective-permute-start | bytes 786440 | tf_op jit(solution)/shard_map/ppermute | solution.py:139
  209.0 21.1 %collective-permute-start.36 = (bf16[2,2,2,128,128]{4,3,2,1,0:T(8,128)(2,1)S(1)}, bf16[2,2,2,128,128]{4,3,2,1,0:T(8,128)(2,1)S(1)}, u32[]{:S(2)}, u32[]{:S(2)}) collective-permute-start(bf16[2,2,2,128,128]{4,3,2,1,0:T(8,128)(2,1)S(1)} %add_convert_fusion.1), channel_id=1, source_target_pairs={{4,0},{9,1},{6,2},{11,3},{20,16},{25,17},{22,18},{27,19}} | collective-permute-start | bytes 786440 | tf_op jit(solution)/shard_map/ppermute | solution.py:131
  211.4 21.6 %collective-permute-start.32 = (bf16[2,2,2,128,128]{4,3,2,1,0:T(8,128)(2,1)S(1)}, bf16[2,2,2,128,128]{4,3,2,1,0:T(8,128)(2,1)S(1)}, u32[]{:S(2)}, u32[]{:S(2)}) collective-permute-start(bf16[2,2,2,128,128]{4,3,2,1,0:T(8,128)(2,1)S(1)} %add_convert_fusion.2), channel_id=1, source_target_pairs={{4,0},{9,1},{6,2},{11,3},{20,16},{25,17},{22,18},{27,19}} | collective-permute-start | bytes 786440 | tf_op jit(solution)/shard_map/ppermute | solution.py:131
  213.7 22.1 %collective-permute-start.28 = (bf16[2,2,2,128,128]{4,3,2,1,0:T(8,128)(2,1)S(1)}, bf16[2,2,2,128,128]{4,3,2,1,0:T(8,128)(2,1)S(1)}, u32[]{:S(2)}, u32[]{:S(2)}) collective-permute-start(bf16[2,2,2,128,128]{4,3,2,1,0:T(8,128)(2,1)S(1)} %add_convert_fusion.3), channel_id=1, source_target_pairs={{4,0},{9,1},{6,2},{11,3},{20,16},{25,17},{22,18},{27,19}} | collective-permute-start | bytes 786440 | tf_op jit(solution)/shard_map/ppermute | solution.py:131
  216.0 22.6 %collective-permute-start.24 = (bf16[2,2,2,128,128]{4,3,2,1,0:T(8,128)(2,1)S(1)}, bf16[2,2,2,128,128]{4,3,2,1,0:T(8,128)(2,1)S(1)}, u32[]{:S(2)}, u32[]{:S(2)}) collective-permute-start(bf16[2,2,2,128,128]{4,3,2,1,0:T(8,128)(2,1)S(1)} %add_convert_fusion.4), channel_id=1, source_target_pairs={{4,0},{9,1},{6,2},{11,3},{20,16},{25,17},{22,18},{27,19}} | collective-permute-start | bytes 786440 | tf_op jit(solution)/shard_map/ppermute | solution.py:131
  230.2 8.5 %collective-permute-start.37 = (bf16[2,2,128,128]{3,2,1,0:T(8,128)(2,1)S(1)}, bf16[2,2,128,128]{3,2,1,0:T(8,128)(2,1)S(1)}, u32[]{:S(2)}, u32[]{:S(2)}) collective-permute-start(bf16[2,2,128,128]{3,2,1,0:T(8,128)(2,1)S(1)} %dynamic-slice_bitcast_fusion.1), channel_id=1, source_target_pairs={{0,1},{1,0},{2,3},{3,2},{4,5},{5,4},{6,7},{7,6},{8,9},{9,8},{10,11... | collective-permute-start | bytes 393224 | tf_op jit(solution)/shard_map/ppermute | solution.py:142
  233.0 5.8 %collective-permute-start.33 = (bf16[2,2,128,128]{3,2,1,0:T(8,128)(2,1)S(1)}, bf16[2,2,128,128]{3,2,1,0:T(8,128)(2,1)S(1)}, u32[]{:S(2)}, u32[]{:S(2)}) collective-permute-start(bf16[2,2,128,128]{3,2,1,0:T(8,128)(2,1)S(1)} %dynamic-slice_bitcast_fusion.2), channel_id=1, source_target_pairs={{0,1},{1,0},{2,3},{3,2},{4,5},{5,4},{6,7},{7,6},{8,9},{9,8},{10,11... | collective-permute-start | bytes 393224 | tf_op jit(solution)/shard_map/ppermute | solution.py:142
  235.8 3.0 %collective-permute-start.29 = (bf16[2,2,128,128]{3,2,1,0:T(8,128)(2,1)S(1)}, bf16[2,2,128,128]{3,2,1,0:T(8,128)(2,1)S(1)}, u32[]{:S(2)}, u32[]{:S(2)}) collective-permute-start(bf16[2,2,128,128]{3,2,1,0:T(8,128)(2,1)S(1)} %dynamic-slice_bitcast_fusion.3), channel_id=1, source_target_pairs={{0,1},{1,0},{2,3},{3,2},{4,5},{5,4},{6,7},{7,6},{8,9},{9,8},{10,11... | collective-permute-start | bytes 393224 | tf_op jit(solution)/shard_map/ppermute | solution.py:142
  (21 other events, 89.0 us)
